TPU v7x, 32 devices: a whole 2x2x4 slice. The times are simulated.
32 devices in a mesh: grp: 2 (over y), tile: 4 (over z), rep: 4 (over x, core).
Axes of the slice: x: 2, y: 2, z: 4, core: 2. Of those that a mesh axis runs over, the one named last changes fastest.
Arguments:
- focusing: bfloat16 [2, 512, 1024], P(None, 'grp', 'tile'), parts along dimension 1, may hold values from -6 to 6
- source_basis: bfloat16 [2, 64, 8, 1024], P(None, 'rep', 'grp', 'tile'), parts along dimension 2, may hold values from -0.375 to 0.375
- receiver_basis: bfloat16 [2, 64, 8, 1024], P(None, 'rep', 'grp', 'tile'), parts along dimension 2, may hold values from -0.21875 to 0.21875
- tile_ranks: int32 [8, 4], P('grp', 'tile'), parts along dimension 0, may hold values from 1 to 4
- keep_counts: int32 [8], P(('grp', 'tile')), parts along dimension 0, may hold values from 64 to 256
Outputs:
- forward_data: float32 [2, 512, 1024], P(None, ('grp', 'rep'), 'tile'), parts along dimension 1
- muted_adjoint_result: float32 [2, 512, 1024], P(None, ('grp', 'rep'), 'tile'), parts along dimension 1
- correlations: float32 [2, 256, 512], P(None, 'rep', 'grp'), parts along dimension 2
There are 2 independent parts, one for each index of `grp`. A program takes and returns all parts, laid end to end along the dimension named above; each array names one. Nothing has to cross between parts.
Inputs may be any that keep to these rules, and one draw needn't show every extreme that they name: `tile_ranks`: number of live buckets of 16 ranks in each tile. `keep_counts`: receivers kept in each receiver tile, counted from its first position.
All inputs are finite; a program needn't handle non-finite values.
Results may differ from a plain program's by a relative error of at most 0.0039.
Values may be sent and summed in bfloat16 or wider, within the bound.
A program may use at most 64 MiB of HBM per device.

v0:
```python
import math

import jax
import jax.numpy as jnp
from jax import lax
from jax.sharding import PartitionSpec as P

SPAN = 256
BUCKET = 16
FOC = 256


def bucket_live(rank_column, local_tile_ranks):
    bucket_index = lax.iota(jnp.int32, local_tile_ranks) // BUCKET
    return bucket_index[:, None] < rank_column[None, :]


def forward_coefficients(basis_here, focal_here, live_mask):
    local_tile_ranks = basis_here.shape[1]
    row_tiles = basis_here.shape[2]
    width_here = basis_here.shape[3]
    points_here = focal_here.shape[1]
    product = lax.dot_general(
        basis_here.reshape(2 * local_tile_ranks * row_tiles, width_here),
        focal_here.reshape(2 * points_here, width_here),
        (((1,), (1,)), ((), ())),
        preferred_element_type=jnp.float32,
    )
    product = product.reshape(2, local_tile_ranks, row_tiles, 2, points_here)
    real_part = product[0, :, :, 0] - product[1, :, :, 1]
    imag_part = product[0, :, :, 1] + product[1, :, :, 0]
    stacked = jnp.where(live_mask[None, :, :, None], jnp.stack([real_part, imag_part]), 0.0)
    return stacked.astype(jnp.bfloat16).reshape(2, local_tile_ranks, row_tiles, 1, points_here)


def forward_regroup(coefficient, lifting):
    local_tile_ranks = lifting.shape[1]
    col_tiles = lifting.shape[2]
    width_here = lifting.shape[3]
    flattened_lifting = lifting.reshape(2, local_tile_ranks * col_tiles, width_here)
    arrived = lax.all_to_all(coefficient, "tile", split_axis=2, concat_axis=3, tiled=True)
    item_count = arrived.shape[4]
    received_flattened = arrived.reshape(2, local_tile_ranks * col_tiles, item_count)
    blocks = jnp.einsum(
        "wgh,lgj->wlhj", received_flattened, flattened_lifting, preferred_element_type=jnp.float32
    )
    return jnp.stack([blocks[0, 0] - blocks[1, 1], blocks[1, 0] + blocks[0, 1]])


def adjoint_coefficients(lifting, masked):
    local_tile_ranks = lifting.shape[1]
    col_tiles = lifting.shape[2]
    width_here = lifting.shape[3]
    points_here = masked.shape[1]
    blocks = jnp.einsum(
        "pks,qfs->pqkf",
        lifting.reshape(2, local_tile_ranks * col_tiles, width_here),
        masked,
        preferred_element_type=jnp.float32,
    )
    stacked = jnp.stack([blocks[0, 0] + blocks[1, 1], blocks[0, 1] - blocks[1, 0]])
    return stacked.astype(jnp.bfloat16).reshape(2, local_tile_ranks, 1, col_tiles, points_here)


def adjoint_regroup(coefficient, basis_here, live_mask):
    local_tile_ranks = basis_here.shape[1]
    row_tiles = basis_here.shape[2]
    width_here = basis_here.shape[3]
    flattened_basis = basis_here.reshape(2, local_tile_ranks * row_tiles, width_here)
    arrived = lax.all_to_all(coefficient, "tile", split_axis=3, concat_axis=2, tiled=True)
    item_count = arrived.shape[4]
    kept_rows = jnp.where(live_mask[None, :, :, None, None], arrived, jnp.zeros((), jnp.bfloat16))
    received_flattened = kept_rows.reshape(2, local_tile_ranks * row_tiles, item_count)
    blocks = jnp.einsum(
        "wgh,lgj->wlhj", received_flattened, flattened_basis, preferred_element_type=jnp.float32
    )
    return jnp.stack([blocks[0, 0] + blocks[1, 1], blocks[1, 0] - blocks[0, 1]])


def correlate(image_part, focusing, factor):
    blocks = jnp.einsum(
        "pgs,qfs->pqgf",
        image_part,
        focusing.astype(jnp.float32),
        precision=lax.Precision.HIGHEST,
        preferred_element_type=jnp.float32,
    )
    return factor * jnp.stack([blocks[0, 0] + blocks[1, 1], blocks[1, 0] - blocks[0, 1]])


def per_device(focusing, source_basis, receiver_basis, tile_ranks, keep_counts):
    width_here = focusing.shape[2]
    portion_count = FOC // lax.axis_size("rep")
    rep_index = lax.axis_index("rep")
    column = tile_ranks[:, 0]
    weights = (lax.iota(jnp.int32, width_here) < keep_counts[0]).astype(jnp.float32)
    order_total = width_here * lax.axis_size("tile")
    factor = 1.0 / math.sqrt(SPAN * order_total)
    every_source, receiver_all = (
        lax.all_gather(source_basis, "rep", axis=1, tiled=True),
        lax.all_gather(receiver_basis, "rep", axis=1, tiled=True),
    )
    focal_share = lax.dynamic_slice_in_dim(focusing, rep_index * portion_count, portion_count, 1)
    live_mask = bucket_live(column, every_source.shape[1])
    coefficient = forward_coefficients(every_source, focal_share, live_mask)
    forward_data = forward_regroup(coefficient, receiver_all)
    masked = (forward_data * weights).astype(jnp.bfloat16)
    muted_adjoint_result = adjoint_regroup(
        adjoint_coefficients(receiver_all, masked), every_source, live_mask
    )
    correlations = lax.psum(correlate(muted_adjoint_result, focusing, factor), "tile")
    return (forward_data, muted_adjoint_result, correlations)


def solution(mesh):
    placed = (
        P(None, "grp", "tile"),
        P(None, "rep", "grp", "tile"),
        P(None, "rep", "grp", "tile"),
        P("grp", "tile"),
        P(("grp", "tile")),
    )
    return jax.shard_map(
        per_device,
        mesh=mesh,
        in_specs=placed,
        out_specs=(
            P(None, ("grp", "rep"), "tile"),
            P(None, ("grp", "rep"), "tile"),
            P(None, "rep", "grp"),
        ),
        check_vma=False,
    )
```

profile of v0, /device:TPU:0, one launch (start us, length us, event | category | flops | bytes accessed | tf_op | source)
XLA Modules:
  0.0 86.4 jit_solution(12190605883118274594)
XLA Ops:
  7.2 7.5 %all_gather.6 = bf16[2,64,4,256]{3,2,1,0:T(4,128)(2,1)S(1)} all-gather(bf16[2,16,4,256]{3,2,1,0:T(4,128)(2,1)} %param.6), channel_id=1, replica_groups=mesh['grp'=2,'tile'=4,'rep'=4] {'rep'}, dimensions={1}, use_global_device_ids=true | all-gather | bytes 327680 | tf_op jit(solution)/shard_map/all_gather | solution.py:100
  14.8 0.2 convolution_bitcast_fusion.4
  15.1 0.1 copy.25
  15.2 0.3 reshape.368
  15.5 0.3 slice_subtract_fusion
  15.8 0.6 copy-done.4
  16.7 0.5 fusion
  17.3 0.8 reshape.381
  18.1 5.0 %all-to-all-start = ((bf16[4,2,4096]{2,1,0:T(2,128)(2,1)}), bf16[4,2,4096]{2,1,0:T(2,128)(2,1)S(1)}, u32[]{:S(2)}, u32[]{:S(2)}) async-start(bf16[4,2,4096]{2,1,0:T(2,128)(2,1)} %reshape.381), calls=%async_computation | async-start | bytes 131072 | tf_op jit(solution)/shard_map/all_to_all | solution.py:41
  23.1 5.8 %all_gather.7 = bf16[2,64,4,256]{3,2,1,0:T(4,128)(2,1)S(1)} all-gather(bf16[2,16,4,256]{3,2,1,0:T(4,128)(2,1)S(1)} %copy-done.3), channel_id=1, replica_groups=mesh['grp'=2,'tile'=4,'rep'=4] {'rep'}, dimensions={1}, use_global_device_ids=true | all-gather | bytes 327680 | tf_op jit(solution)/shard_map/all_gather | solution.py:101
  29.6 0.1 reshape.382
  29.9 0.2 convolution_bitcast_fusion.2
  30.2 0.2 convolution_bitcast_fusion.3
  30.4 0.4 copy-done.1
  31.2 0.8 reshape.383
  32.0 5.1 %all-to-all-start.1 = ((bf16[4,2,4096]{2,1,0:T(2,128)(2,1)}), bf16[4,2,4096]{2,1,0:T(2,128)(2,1)S(1)}, u32[]{:S(2)}, u32[]{:S(2)}) async-start(bf16[4,2,4096]{2,1,0:T(2,128)(2,1)} %reshape.383), calls=%async_computation.1 | async-start | bytes 131072 | tf_op jit(solution)/shard_map/all_to_all | solution.py:70
  37.2 5.7 %all-to-all-done.1 = bf16[4,2,4096]{2,1,0:T(2,128)(2,1)S(1)} async-done(((bf16[4,2,4096]{2,1,0:T(2,128)(2,1)}), bf16[4,2,4096]{2,1,0:T(2,128)(2,1)S(1)}, u32[]{:S(2)}, u32[]{:S(2)}) %all-to-all-start.1) | async-done | bytes 65568 | tf_op jit(solution)/shard_map/all_to_all | solution.py:70
  42.8 0.1 reshape.384
  43.2 0.2 convolution_bitcast_fusion.1
  43.5 0.4 convolution_bitcast_fusion
  43.9 0.2 copy-done.2
  44.1 0.7 maximum_multiply_fusion
  44.8 33.2 %all-reduce.2.cloned.1.call-done = f32[2,64,256]{2,1,0:T(8,128)} async-done(((f32[2,64,256]{2,1,0:T(8,128)}), f32[2,64,256]{2,1,0:T(8,128)}) %all-reduce.2.cloned.1.call-update) | async-done | bytes 131088 | tf_op jit(solution)/shard_map/psum | solution.py:111
  78.0 1.6 %copy.48 = f32[2,64,256]{2,1,0:T(8,128)} copy(f32[2,64,256]{2,1,0:T(8,128)} %all-reduce.2.cloned.1.call-done) | data formatting | bytes 262144
  (32 shorter events, 1.3 us)
Async XLA Ops:
  7.2 7.6 %copy-start = (bf16[2,256,256]{2,1,0:T(8,128)(2,1)S(1)}, bf16[2,256,256]{2,1,0:T(8,128)(2,1)}, u32[]{:S(2)}) copy-start(bf16[2,256,256]{2,1,0:T(8,128)(2,1)} %param.5) | copy-start | bytes 786436
  15.8 0.7 copy-start.4
  18.1 5.0 %copy-start.3 = (bf16[2,16,4,256]{3,2,1,0:T(4,128)(2,1)S(1)}, bf16[2,16,4,256]{3,2,1,0:T(4,128)(2,1)}, u32[]{:S(2)}) copy-start(bf16[2,16,4,256]{3,2,1,0:T(4,128)(2,1)} %param.7) | copy-start | bytes 196612
  18.1 11.6 %all-to-all-start = ((bf16[4,2,4096]{2,1,0:T(2,128)(2,1)}), bf16[4,2,4096]{2,1,0:T(2,128)(2,1)S(1)}, u32[]{:S(2)}, u32[]{:S(2)}) async-start(bf16[4,2,4096]{2,1,0:T(2,128)(2,1)} %reshape.381), calls=%async_computation | async-start | bytes 131072 | tf_op jit(solution)/shard_map/all_to_all | solution.py:41
  30.1 0.7 copy-start.1
  32.0 10.8 %all-to-all-start.1 = ((bf16[4,2,4096]{2,1,0:T(2,128)(2,1)}), bf16[4,2,4096]{2,1,0:T(2,128)(2,1)S(1)}, u32[]{:S(2)}, u32[]{:S(2)}) async-start(bf16[4,2,4096]{2,1,0:T(2,128)(2,1)} %reshape.383), calls=%async_computation.1 | async-start | bytes 131072 | tf_op jit(solution)/shard_map/all_to_all | solution.py:70
  37.1 40.9 %all-reduce.2.cloned.1.call-start = ((), (), s32[]{:S(2)}) async-start(), calls=%async_computation.2 | async-start | bytes 262144 | tf_op jit(solution)/shard_map/psum | solution.py:111
  43.5 0.7 copy-start.2
Sparse Core Ops, SparseCore 0:
  45.0 32.9 all-reduce.1
where the time goes:
time: 86.9 us; the launch traced here: 86.4 us
  waiting for transfers between devices  38.9 us (45%)
  between operations  14.9 us (17%)
  blocking collectives  13.3 us (15%)
  starting transfers between devices  10.1 us (12%)
  local copies, waits for them, and re-layouts  6.04 us (7%)
  other arithmetic  1.89 us (2%)
  matrix products  1.24 us (1%)
    psum x1, waiting for transfers between devices, per_device(): lax.psum(correlate(muted_adjoint_result, focusing, factor), 'tile')  33.2 us
    all_gather x1, blocking collectives, per_device(): lax.all_gather(source_basis, 'rep', axis=1, tiled=True)  7.54 us
    all_gather x1, blocking collectives, per_device(): lax.all_gather(receiver_basis, 'rep', axis=1, tiled=True)  5.77 us
    all_to_all x1, waiting for transfers between devices, adjoint_regroup(): lax.all_to_all(coefficient, 'tile', split_axis=3, concat_axis=2, tiled=True)  5.67 us
    all_to_all x1, starting transfers between devices, adjoint_regroup(): lax.all_to_all(coefficient, 'tile', split_axis=3, concat_axis=2, tiled=True)  5.09 us
    all_to_all x1, starting transfers between devices, forward_regroup(): lax.all_to_all(coefficient, 'tile', split_axis=2, concat_axis=3, tiled=True)  5.05 us
    unnamed x15, local copies, waits for them, and re-layouts  4.78 us
  transfers between devices with their start and end apart: 3, of which 2 were waited for; matrix products, arithmetic and copies ran while one was open for 0% of the time, Pallas kernels for 0%

commit v1 on v0

v1 whole, which is shorter than its diff:
```python
import functools
import math

import jax
import jax.numpy as jnp
from jax import lax
from jax.experimental import pallas as pl
from jax.experimental.pallas import tpu as pltpu
from jax.sharding import PartitionSpec as P

SPAN = 256
BUCKET = 16
FOC = 256
MESH = pl.DeviceIdType.MESH

NT = (((1,), (1,)), ((), ()))
TN = (((0,), (0,)), ((), ()))


def dot(a, b, dims):
    return lax.dot_general(a, b, dims, preferred_element_type=jnp.float32)


def each(first, last, body):
    if last - first <= 16:
        for i in range(first, last):
            body(i)
    else:
        pl.loop(first, last)(body)


def kernel(tiles, reps, reduce_here, factor, foc_ref, sb_ref, rb_ref, keep_ref,
           fwd_ref, mar_ref, cor_ref,
           rb_all, sb_all, coef_out, coef_in, back_out, back_in, red_out, red_in, cor_all,
           coef_send, coef_recv, rb_send, rb_recv, sb_send, sb_recv,
           back_send, back_recv, red_send, red_recv, cor_send, cor_recv):
    t = lax.axis_index("tile")
    r = lax.axis_index("rep")
    me = t * reps + r
    count = tiles * reps
    ranks, span = sb_ref.shape[2], sb_ref.shape[3]
    share = foc_ref.shape[1] // reps
    rows = reps * tiles * ranks

    def peer(d):
        other = lax.rem(me + d, count)
        return other // reps, lax.rem(other, reps)

    barrier = pltpu.get_barrier_semaphore()

    def greet(d):
        pt, pr = peer(d)
        pl.semaphore_signal(barrier, inc=1, device_id={"tile": pt, "rep": pr}, device_id_type=MESH)

    each(1, count, greet)

    shares, turned = [], []
    for j in range(reps):
        re = foc_ref[0, j * share:(j + 1) * share, :]
        im = foc_ref[1, j * share:(j + 1) * share, :]
        shares += [re, im]
        turned += [-im, re]
    coef = dot(sb_ref[0].reshape(tiles * ranks, span), jnp.concatenate(shares, 0), NT)
    coef += dot(sb_ref[1].reshape(tiles * ranks, span), jnp.concatenate(turned, 0), NT)
    coef = coef.astype(jnp.bfloat16).reshape(tiles, ranks, reps * 2 * share)
    for j in range(reps):
        coef_out[j] = coef[:, :, j * 2 * share:(j + 1) * 2 * share]

    pl.semaphore_wait(barrier, count - 1)

    def basis_copy(src, dst, send, recv, d):
        return pltpu.make_async_remote_copy(
            src_ref=src, dst_ref=dst.at[r], send_sem=send.at[d], recv_sem=recv.at[d],
            device_id={"tile": t, "rep": lax.rem(r + d, reps)}, device_id_type=MESH)

    def coef_copy(d):
        pt, pr = peer(d)
        return pltpu.make_async_remote_copy(
            src_ref=coef_out.at[pr, pt], dst_ref=coef_in.at[r, t],
            send_sem=coef_send.at[d], recv_sem=coef_recv.at[d],
            device_id={"tile": pt, "rep": pr}, device_id_type=MESH)

    def tile_copy(src, dst, send, recv, d):
        return pltpu.make_async_remote_copy(
            src_ref=src, dst_ref=dst, send_sem=send.at[d], recv_sem=recv.at[d],
            device_id={"tile": lax.rem(t + d, tiles), "rep": r}, device_id_type=MESH)

    rb_copies = [basis_copy(rb_ref, rb_all, rb_send, rb_recv, d) for d in range(1, reps)]
    sb_copies = [basis_copy(sb_ref, sb_all, sb_send, sb_recv, d) for d in range(1, reps)]
    each(1, count, lambda d: coef_copy(d).start())
    for c in rb_copies:
        c.start()
    for c in sb_copies:
        c.start()
    rb_all[r] = rb_ref[...]
    sb_all[r] = sb_ref[...]
    coef_in[r, t] = coef_out[r, t]

    for c in rb_copies:
        c.wait_recv()
    each(1, count, lambda d: coef_copy(d).wait_recv())

    arrived = coef_in[...].reshape(rows, 2 * share)
    rre = rb_all[:, 0].reshape(rows, span)
    rim = rb_all[:, 1].reshape(rows, span)
    g0 = dot(arrived, rre, TN)
    g1 = dot(arrived, rim, TN)
    fre = g0[:share] - g1[share:]
    fim = g0[share:] + g1[:share]
    fwd_ref[0] = fre
    fwd_ref[1] = fim
    kept = lax.broadcasted_iota(jnp.int32, (share, span), 1) < keep_ref[0]
    mre = jnp.where(kept, fre, 0.0).astype(jnp.bfloat16)
    mim = jnp.where(kept, fim, 0.0).astype(jnp.bfloat16)
    back = dot(rre, jnp.concatenate([mre, mim], 0), NT)
    back += dot(rim, jnp.concatenate([mim, -mre], 0), NT)
    back_out[...] = back.astype(jnp.bfloat16).reshape(reps, tiles, ranks, 2 * share)

    def back_copy(d):
        return tile_copy(back_out.at[:, lax.rem(t + d, tiles)], back_in.at[:, t], back_send, back_recv, d)

    each(1, tiles, lambda d: back_copy(d).start())
    back_in[:, t] = back_out[:, t]
    for c in sb_copies:
        c.wait_recv()
    each(1, tiles, lambda d: back_copy(d).wait_recv())

    arrived = back_in[...].reshape(rows, 2 * share)
    h0 = dot(arrived, sb_all[:, 0].reshape(rows, span), TN)
    h1 = dot(arrived, sb_all[:, 1].reshape(rows, span), TN)
    are = h0[:share] + h1[share:]
    aim = h0[share:] - h1[:share]
    mar_ref[0] = are
    mar_ref[1] = aim

    are = are.astype(jnp.bfloat16)
    aim = aim.astype(jnp.bfloat16)
    part_re = dot(are, foc_ref[0], NT) + dot(aim, foc_ref[1], NT)
    part_im = dot(aim, foc_ref[0], NT) - dot(are, foc_ref[1], NT)
    if reduce_here:
        part = jnp.concatenate([part_re, part_im], 0).astype(jnp.bfloat16)
        red_out[...] = part.reshape(red_out.shape)

        def red_copy(d):
            return tile_copy(red_out.at[lax.rem(t + d, tiles)], red_in.at[t], red_send, red_recv, d)

        def cor_copy(d):
            return tile_copy(cor_all.at[t], cor_all.at[t], cor_send, cor_recv, d)

        each(1, tiles, lambda d: red_copy(d).start())
        red_in[t] = red_out[t]
        each(1, tiles, lambda d: red_copy(d).wait_recv())
        total = red_in[0].astype(jnp.float32)
        for j in range(1, tiles):
            total += red_in[j].astype(jnp.float32)
        cor_all[t] = (factor * total).astype(jnp.bfloat16)
        each(1, tiles, lambda d: cor_copy(d).start())
        each(1, tiles, lambda d: cor_copy(d).wait_recv())
        cor_ref[...] = cor_all[...].astype(jnp.float32).reshape(cor_ref.shape)
        each(1, tiles, lambda d: red_copy(d).wait_send())
        each(1, tiles, lambda d: cor_copy(d).wait_send())
    else:
        cor_ref[0] = factor * part_re
        cor_ref[1] = factor * part_im

    each(1, count, lambda d: coef_copy(d).wait_send())
    for c in rb_copies + sb_copies:
        c.wait_send()
    each(1, tiles, lambda d: back_copy(d).wait_send())


def per_device(focusing, source_basis, receiver_basis, tile_ranks, keep_counts):
    tiles, reps = lax.axis_size("tile"), lax.axis_size("rep")
    _, ranks, _, span = source_basis.shape
    points = focusing.shape[1]
    share = points // reps
    factor = 1.0 / math.sqrt(SPAN * span * tiles)
    first = lax.axis_index("rep") * ranks
    live = (first + lax.iota(jnp.int32, ranks))[:, None] // BUCKET < tile_ranks[:, 0][None, :]
    sb = jnp.where(live[None, :, :, None], source_basis, jnp.zeros((), jnp.bfloat16))
    sb = jnp.transpose(sb, (0, 2, 1, 3))
    rb = jnp.transpose(receiver_basis, (0, 2, 1, 3))
    reduce_here = (2 * share) % (16 * tiles) == 0
    chunk = 2 * share // tiles if reduce_here else 16
    bf = jnp.bfloat16
    dma = pltpu.SemaphoreType.DMA
    vmem = pl.BlockSpec(memory_space=pltpu.VMEM)
    fwd, mar, cor = pl.pallas_call(
        functools.partial(kernel, tiles, reps, reduce_here, factor),
        out_shape=(
            jax.ShapeDtypeStruct((2, share, span), jnp.float32),
            jax.ShapeDtypeStruct((2, share, span), jnp.float32),
            jax.ShapeDtypeStruct((2, share, points), jnp.float32),
        ),
        in_specs=[vmem, vmem, vmem, pl.BlockSpec(memory_space=pltpu.SMEM)],
        out_specs=(vmem, vmem, vmem),
        scratch_shapes=[
            pltpu.VMEM((reps, 2, tiles, ranks, span), bf),
            pltpu.VMEM((reps, 2, tiles, ranks, span), bf),
            pltpu.VMEM((reps, tiles, ranks, 2 * share), bf),
            pltpu.VMEM((reps, tiles, ranks, 2 * share), bf),
            pltpu.VMEM((reps, tiles, ranks, 2 * share), bf),
            pltpu.VMEM((reps, tiles, ranks, 2 * share), bf),
            pltpu.VMEM((tiles, chunk, points), bf),
            pltpu.VMEM((tiles, chunk, points), bf),
            pltpu.VMEM((tiles, chunk, points), bf),
            dma((tiles * reps,)), dma((tiles * reps,)),
            dma((reps,)), dma((reps,)), dma((reps,)), dma((reps,)),
            dma((tiles,)), dma((tiles,)), dma((tiles,)), dma((tiles,)), dma((tiles,)), dma((tiles,)),
        ],
        compiler_params=pltpu.CompilerParams(
            collective_id=0, has_side_effects=True, vmem_limit_bytes=56 * 2 ** 20),
    )(focusing, sb, rb, keep_counts)
    if not reduce_here:
        cor = lax.psum(cor, "tile")
    return fwd, mar, cor


def solution(mesh):
    placed = (
        P(None, "grp", "tile"),
        P(None, "rep", "grp", "tile"),
        P(None, "rep", "grp", "tile"),
        P("grp", "tile"),
        P(("grp", "tile")),
    )
    return jax.shard_map(
        per_device,
        mesh=mesh,
        in_specs=placed,
        out_specs=(
            P(None, ("grp", "rep"), "tile"),
            P(None, ("grp", "rep"), "tile"),
            P(None, "rep", "grp"),
        ),
        check_vma=False,
    )
```

time: 86.9 us -> 31.8 us (0.37)
  waiting for transfers between devices: 38.9 us -> 0 us
  Pallas kernels: 0 us -> 24.7 us
  between operations: 14.9 us -> 1.31 us
  blocking collectives: 13.3 us -> 0 us
  starting transfers between devices: 10.1 us -> 0 us
  local copies, waits for them, and re-layouts: 6.04 us -> 3.86 us
  matrix products: 1.24 us -> 0 us
    psum x1 -> x0, waiting for transfers between devices: 33.2 us -> none  [per_device(): lax.psum(correlate(muted_adjoint_result, focusing, factor), 'tile')]
    pallas_call x0 -> x1, Pallas kernels: none -> 24.7 us  [per_device(): pl.pallas_call(functools.partial(kernel, tiles, reps, reduce_here, factor...]
    all_gather x2 -> x0, blocking collectives: 13.3 us -> none  [the longest x1 7.54 us: per_device(): lax.all_gather(source_basis, 'rep', axis=1, tiled=True)]
    all_to_all x2 -> x0, starting transfers between devices: 10.1 us -> none  [the longest x1 5.09 us: adjoint_regroup(): lax.all_to_all(coefficient, 'tile', split_axis=3, concat_axis=2, tiled=True)]
    all_to_all x2 -> x0, waiting for transfers between devices: 5.68 us -> none  [the longest x1 5.67 us: adjoint_regroup(): lax.all_to_all(coefficient, 'tile', split_axis=3, concat_axis=2, tiled=True)]
    transpose x0 -> x1, other arithmetic: none -> 1.58 us  [per_device(): rb = jnp.transpose(receiver_basis, (0, 2, 1, 3))]
    dot_general x5 -> x0, matrix products: 1.24 us -> none  [the longest x1 0.4 us: correlate(): jnp.einsum('pgs,qfs->pqgf', image_part, focusing.astype(jnp.float32), pre...]
    unnamed x15 -> x9, local copies, waits for them, and re-layouts: 4.78 us -> 3.86 us
  transfers between devices with their start and end apart: 3 -> 0, of which waited for: 2 -> 0; matrix products, arithmetic and copies ran while one was open for 0% -> 0% of each run, Pallas kernels for 0% -> 0%
where the time goes in v1:
time: 31.8 us; the launch traced here: 31.5 us
  Pallas kernels  24.7 us (78%)
  local copies, waits for them, and re-layouts  3.86 us (12%)
  other arithmetic  1.66 us (5%)
  between operations  1.31 us (4%)
    pallas_call x1, Pallas kernels, per_device(): pl.pallas_call(functools.partial(kernel, tiles, reps, reduce_here, factor...  24.7 us
    unnamed x9, local copies, waits for them, and re-layouts  3.86 us
    transpose x1, other arithmetic, per_device(): rb = jnp.transpose(receiver_basis, (0, 2, 1, 3))  1.58 us

profile of v1, /device:TPU:0, one launch (start us, length us, event | category | flops | bytes accessed | tf_op | source)
XLA Modules:
  0.0 31.5 jit_solution(12463928015747481725)
XLA Ops:
  1.3 0.0 copy-start.2
  1.3 0.6 %copy-done.2 = s32[4,1]{0,1:T(1,128)S(1)} copy-done((s32[4,1]{0,1:T(1,128)S(1)}, s32[4,1]{0,1:T(1,128)}, u32[]{:S(2)}) %copy-start.2) | copy-done | bytes 40
  2.0 0.1 broadcast_compare_fusion
  2.0 1.6 %copy_bitcast_fusion = (bf16[2,4,16,256]{3,2,1,0:T(8,128)(2,1)}, bf16[2,4,16,256]{3,2,1,0:T(8,128)(2,1)}) fusion(bf16[2,16,4,256]{3,2,1,0:T(4,128)(2,1)} %param.7, bf16[2,16,4,256]{3,2,1,0:T(4,128)(2,1)} %param.6, pred[16,4]{0,1:T(4,128)(4,1)S(1)} %broadcast_compare_fusion), kind=kLoop, calls=%fused_computation | loop fusion | flops 32768 | bytes 262208 | tf_op jit(solution)/shard_map/transpose | solution.py:182
  3.6 24.7 %shard_map.76 = (f32[2,64,256]{2,1,0:T(8,128)}, f32[2,64,256]{2,1,0:T(8,128)}, f32[2,64,256]{2,1,0:T(8,128)}) custom-call(bf16[2,256,256]{2,1,0:T(8,128)(2,1)} %foc_ref.1, bf16[2,4,16,256]{3,2,1,0:T(8,128)(2,1)} %get-tuple-element.4.sb_ref, bf16[2,4,16,256]{3,2,1,0:T(8,128)(2,1)} %get-tuple-element.3.rb_ref, s32[1]{0:T(128)S(6)} %copy.17.keep_ref), custom_call_target="tpu_custom_call" | custom-call | tf_op jit(solution)/shard_map/pallas_call | solution.py:188
  28.3 0.0 copy-start.1
  28.3 1.6 %copy.18 = f32[2,64,256]{2,1,0:T(8,128)} copy(f32[2,64,256]{2,1,0:T(8,128)} %get-tuple-element.8) | data formatting | bytes 262144
  29.9 0.0 copy-done.1
  29.9 0.0 copy-start
  29.9 0.7 %copy.19 = f32[2,64,256]{2,1,0:T(8,128)} copy(f32[2,64,256]{2,1,0:T(8,128)S(1)} %copy-done.1) | data formatting | bytes 262144
  30.6 0.3 copy-done
  30.9 0.7 %copy.20 = f32[2,64,256]{2,1,0:T(8,128)} copy(f32[2,64,256]{2,1,0:T(8,128)S(1)} %copy-done) | data formatting | bytes 262144
  (1 shorter events, 0.0 us)
Async XLA Ops:
  1.3 0.7 %copy-start.2 = (s32[4,1]{0,1:T(1,128)S(1)}, s32[4,1]{0,1:T(1,128)}, u32[]{:S(2)}) copy-start(s32[4,1]{0,1:T(1,128)} %param.8) | copy-start | bytes 52
  28.3 1.6 %copy-start.1 = (f32[2,64,256]{2,1,0:T(8,128)S(1)}, f32[2,64,256]{2,1,0:T(8,128)}, u32[]{:S(2)}) copy-start(f32[2,64,256]{2,1,0:T(8,128)} %get-tuple-element.9) | copy-start | bytes 393220
  29.9 1.0 %copy-start = (f32[2,64,256]{2,1,0:T(8,128)S(1)}, f32[2,64,256]{2,1,0:T(8,128)}, u32[]{:S(2)}) copy-start(f32[2,64,256]{2,1,0:T(8,128)} %get-tuple-element.10) | copy-start | bytes 393220

commit v2 on v1

--- a/solution.py
+++ b/solution.py
@@ -29,9 +29,9 @@
         pl.loop(first, last)(body)
 
 
-def kernel(tiles, reps, reduce_here, factor, foc_ref, sb_ref, rb_ref, keep_ref,
+def kernel(tiles, reps, reduce_here, factor, foc_ref, source_ref, receiver_ref, ranks_ref, keep_ref,
            fwd_ref, mar_ref, cor_ref,
-           rb_all, sb_all, coef_out, coef_in, back_out, back_in, red_out, red_in, cor_all,
+           sb_ref, rb_ref, rb_all, sb_all, coef_out, coef_in, back_out, back_in, red_out, red_in, cor_all,
            coef_send, coef_recv, rb_send, rb_recv, sb_send, sb_recv,
            back_send, back_recv, red_send, red_recv, cor_send, cor_recv):
     t = lax.axis_index("tile")
@@ -53,6 +53,12 @@
         pl.semaphore_signal(barrier, inc=1, device_id={"tile": pt, "rep": pr}, device_id_type=MESH)
 
     each(1, count, greet)
+
+    bucket = (r * ranks + lax.broadcasted_iota(jnp.int32, (2, ranks, span), 1)) // BUCKET
+    for a in range(tiles):
+        wide = source_ref[:, :, a, :].astype(jnp.float32)
+        sb_ref[:, a] = jnp.where(bucket < ranks_ref[a], wide, 0.0).astype(jnp.bfloat16)
+        rb_ref[:, a] = receiver_ref[:, :, a, :]
 
     shares, turned = [], []
     for j in range(reps):
@@ -68,10 +74,38 @@
 
     pl.semaphore_wait(barrier, count - 1)
 
-    def basis_copy(src, dst, send, recv, d):
-        return pltpu.make_async_remote_copy(
-            src_ref=src, dst_ref=dst.at[r], send_sem=send.at[d], recv_sem=recv.at[d],
-            device_id={"tile": t, "rep": lax.rem(r + d, reps)}, device_id_type=MESH)
+    class Gather:
+        def __init__(self, own, held, send, recv):
+            self.own, self.held, self.send, self.recv = own, held, send, recv
+            if reps == 4:
+                self.first = [self.copy(own, r, r ^ 2, 0), self.copy(own, r, r ^ 1, 1)]
+                self.second = [self.copy(held.at[r ^ 2], r ^ 2, r ^ 1, 2)]
+            else:
+                self.first = [self.copy(own, r, lax.rem(r + d, reps), d - 1) for d in range(1, reps)]
+                self.second = []
+
+        def copy(self, src, slot, to, i):
+            return pltpu.make_async_remote_copy(
+                src_ref=src, dst_ref=self.held.at[slot], send_sem=self.send.at[i], recv_sem=self.recv.at[i],
+                device_id={"tile": t, "rep": to}, device_id_type=MESH)
+
+        def start(self):
+            for c in self.first:
+                c.start()
+            self.held[r] = self.own[...]
+
+        def forward(self):
+            if self.second:
+                self.first[0].wait_recv()
+                self.second[0].start()
+
+        def wait_recv(self):
+            for c in (self.first[1:] if self.second else self.first) + self.second:
+                c.wait_recv()
+
+        def wait_send(self):
+            for c in self.first + self.second:
+                c.wait_send()
 
     def coef_copy(d):
         pt, pr = peer(d)
@@ -85,20 +119,18 @@
             src_ref=src, dst_ref=dst, send_sem=send.at[d], recv_sem=recv.at[d],
             device_id={"tile": lax.rem(t + d, tiles), "rep": r}, device_id_type=MESH)
 
-    rb_copies = [basis_copy(rb_ref, rb_all, rb_send, rb_recv, d) for d in range(1, reps)]
-    sb_copies = [basis_copy(sb_ref, sb_all, sb_send, sb_recv, d) for d in range(1, reps)]
+    rb_gather = Gather(rb_ref, rb_all, rb_send, rb_recv)
+    sb_gather = Gather(sb_ref, sb_all, sb_send, sb_recv)
+    rb_gather.start()
     each(1, count, lambda d: coef_copy(d).start())
-    for c in rb_copies:
-        c.start()
-    for c in sb_copies:
-        c.start()
-    rb_all[r] = rb_ref[...]
-    sb_all[r] = sb_ref[...]
+    sb_gather.start()
     coef_in[r, t] = coef_out[r, t]
 
-    for c in rb_copies:
-        c.wait_recv()
+    rb_gather.forward()
+    rb_gather.wait_recv()
     each(1, count, lambda d: coef_copy(d).wait_recv())
+
+    sb_gather.forward()
 
     arrived = coef_in[...].reshape(rows, 2 * share)
     rre = rb_all[:, 0].reshape(rows, span)
@@ -121,8 +153,7 @@
 
     each(1, tiles, lambda d: back_copy(d).start())
     back_in[:, t] = back_out[:, t]
-    for c in sb_copies:
-        c.wait_recv()
+    sb_gather.wait_recv()
     each(1, tiles, lambda d: back_copy(d).wait_recv())
 
     arrived = back_in[...].reshape(rows, 2 * share)
@@ -164,8 +195,8 @@
         cor_ref[1] = factor * part_im
 
     each(1, count, lambda d: coef_copy(d).wait_send())
-    for c in rb_copies + sb_copies:
-        c.wait_send()
+    rb_gather.wait_send()
+    sb_gather.wait_send()
     each(1, tiles, lambda d: back_copy(d).wait_send())
 
 
@@ -175,15 +206,11 @@
     points = focusing.shape[1]
     share = points // reps
     factor = 1.0 / math.sqrt(SPAN * span * tiles)
-    first = lax.axis_index("rep") * ranks
-    live = (first + lax.iota(jnp.int32, ranks))[:, None] // BUCKET < tile_ranks[:, 0][None, :]
-    sb = jnp.where(live[None, :, :, None], source_basis, jnp.zeros((), jnp.bfloat16))
-    sb = jnp.transpose(sb, (0, 2, 1, 3))
-    rb = jnp.transpose(receiver_basis, (0, 2, 1, 3))
     reduce_here = (2 * share) % (16 * tiles) == 0
     chunk = 2 * share // tiles if reduce_here else 16
     bf = jnp.bfloat16
     dma = pltpu.SemaphoreType.DMA
+    smem = pl.BlockSpec(memory_space=pltpu.SMEM)
     vmem = pl.BlockSpec(memory_space=pltpu.VMEM)
     fwd, mar, cor = pl.pallas_call(
         functools.partial(kernel, tiles, reps, reduce_here, factor),
@@ -192,9 +219,11 @@
             jax.ShapeDtypeStruct((2, share, span), jnp.float32),
             jax.ShapeDtypeStruct((2, share, points), jnp.float32),
         ),
-        in_specs=[vmem, vmem, vmem, pl.BlockSpec(memory_space=pltpu.SMEM)],
+        in_specs=[vmem, vmem, vmem, smem, smem],
         out_specs=(vmem, vmem, vmem),
         scratch_shapes=[
+            pltpu.VMEM((2, tiles, ranks, span), bf),
+            pltpu.VMEM((2, tiles, ranks, span), bf),
             pltpu.VMEM((reps, 2, tiles, ranks, span), bf),
             pltpu.VMEM((reps, 2, tiles, ranks, span), bf),
             pltpu.VMEM((reps, tiles, ranks, 2 * share), bf),
@@ -210,7 +239,7 @@
         ],
         compiler_params=pltpu.CompilerParams(
             collective_id=0, has_side_effects=True, vmem_limit_bytes=56 * 2 ** 20),
-    )(focusing, sb, rb, keep_counts)
+    )(focusing, source_basis, receiver_basis, tile_ranks.reshape(tiles), keep_counts)
     if not reduce_here:
         cor = lax.psum(cor, "tile")
     return fwd, mar, cor

time: 31.8 us -> 29.7 us (0.934)
  other arithmetic: 1.66 us -> 0 us
  local copies, waits for them, and re-layouts: 3.86 us -> 3.21 us
    transpose x1 -> x0, other arithmetic: 1.58 us -> none  [per_device(): rb = jnp.transpose(receiver_basis, (0, 2, 1, 3))]
    unnamed x9 -> x7, local copies, waits for them, and re-layouts: 3.86 us -> 3.21 us
    pallas_call x1, Pallas kernels: 24.7 us -> 25 us  [per_device(): pl.pallas_call(functools.partial(kernel, tiles, reps, reduce_here, factor...]
where the time goes in v2:
time: 29.7 us; the launch traced here: 29.5 us
  Pallas kernels  25 us (84%)
  local copies, waits for them, and re-layouts  3.21 us (11%)
  between operations  1.3 us (4%)
    pallas_call x1, Pallas kernels, per_device(): pl.pallas_call(functools.partial(kernel, tiles, reps, reduce_here, factor...  25 us
    unnamed x7, local copies, waits for them, and re-layouts  3.21 us

profile of v2, /device:TPU:0, one launch (start us, length us, event | category | flops | bytes accessed | tf_op | source)
XLA Modules:
  0.0 29.5 jit_solution(11702444917947673860)
XLA Ops:
  1.3 25.0 %shard_map.76 = (f32[2,64,256]{2,1,0:T(8,128)}, f32[2,64,256]{2,1,0:T(8,128)}, f32[2,64,256]{2,1,0:T(8,128)}) custom-call(bf16[2,256,256]{2,1,0:T(8,128)(2,1)} %foc_ref.1, bf16[2,16,4,256]{3,2,1,0:T(4,128)(2,1)} %source_ref.1, bf16[2,16,4,256]{3,2,1,0:T(4,128)(2,1)} %receiver_ref.1, s32[4]{0:T(128)} %bitcast.1, s32[1]{0:T(128)S(6)} %copy.11.keep_ref), custom_call_target="tpu_custom_call" | custom-call | tf_op jit(solution)/shard_map/pallas_call | solution.py:215
  26.3 0.0 copy-start.1
  26.3 1.6 %copy.12 = f32[2,64,256]{2,1,0:T(8,128)} copy(f32[2,64,256]{2,1,0:T(8,128)} %get-tuple-element.6) | data formatting | bytes 262144
  27.9 0.0 copy-done.1
  27.9 0.0 copy-start
  27.9 0.7 %copy.13 = f32[2,64,256]{2,1,0:T(8,128)} copy(f32[2,64,256]{2,1,0:T(8,128)S(1)} %copy-done.1) | data formatting | bytes 262144
  28.6 0.3 copy-done
  28.9 0.7 %copy.14 = f32[2,64,256]{2,1,0:T(8,128)} copy(f32[2,64,256]{2,1,0:T(8,128)S(1)} %copy-done) | data formatting | bytes 262144
Async XLA Ops:
  26.3 1.6 %copy-start.1 = (f32[2,64,256]{2,1,0:T(8,128)S(1)}, f32[2,64,256]{2,1,0:T(8,128)}, u32[]{:S(2)}) copy-start(f32[2,64,256]{2,1,0:T(8,128)} %get-tuple-element.7) | copy-start | bytes 393220
  27.9 1.0 %copy-start = (f32[2,64,256]{2,1,0:T(8,128)S(1)}, f32[2,64,256]{2,1,0:T(8,128)}, u32[]{:S(2)}) copy-start(f32[2,64,256]{2,1,0:T(8,128)} %get-tuple-element.8) | copy-start | bytes 393220

commit v3 on v2

--- a/solution.py
+++ b/solution.py
@@ -32,6 +32,8 @@
 def kernel(tiles, reps, reduce_here, factor, foc_ref, source_ref, receiver_ref, ranks_ref, keep_ref,
            fwd_ref, mar_ref, cor_ref,
            sb_ref, rb_ref, rb_all, sb_all, coef_out, coef_in, back_out, back_in, red_out, red_in, cor_all,
+           near_out, near_in, near_all,
+           near_send, near_recv, row_send, row_recv,
            coef_send, coef_recv, rb_send, rb_recv, sb_send, sb_recv,
            back_send, back_recv, red_send, red_recv, cor_send, cor_recv):
     t = lax.axis_index("tile")
@@ -119,18 +121,30 @@
             src_ref=src, dst_ref=dst, send_sem=send.at[d], recv_sem=recv.at[d],
             device_id={"tile": lax.rem(t + d, tiles), "rep": r}, device_id_type=MESH)
 
+    def near_copy(d):
+        return tile_copy(near_out.at[lax.rem(t + d, tiles)], near_in.at[t], near_send, near_recv, d)
+
     rb_gather = Gather(rb_ref, rb_all, rb_send, rb_recv)
     sb_gather = Gather(sb_ref, sb_all, sb_send, sb_recv)
+    row_gather = Gather(near_in, near_all, row_send, row_recv)
     rb_gather.start()
     each(1, count, lambda d: coef_copy(d).start())
+    coef_in[r, t] = coef_out[r, t]
+    if reduce_here:
+        fre, fim = foc_ref[0], foc_ref[1]
+        coef = dot(sb_ref[0].reshape(tiles * ranks, span), jnp.concatenate([fre, fim], 0), NT)
+        coef += dot(sb_ref[1].reshape(tiles * ranks, span), jnp.concatenate([-fim, fre], 0), NT)
+        near_out[...] = coef.astype(jnp.bfloat16).reshape(near_out.shape)
+        each(1, tiles, lambda d: near_copy(d).start())
+        near_in[t] = near_out[t]
     sb_gather.start()
-    coef_in[r, t] = coef_out[r, t]
 
     rb_gather.forward()
+    if reduce_here:
+        each(1, tiles, lambda d: near_copy(d).wait_recv())
+        row_gather.start()
     rb_gather.wait_recv()
     each(1, count, lambda d: coef_copy(d).wait_recv())
-
-    sb_gather.forward()
 
     arrived = coef_in[...].reshape(rows, 2 * share)
     rre = rb_all[:, 0].reshape(rows, span)
@@ -141,21 +155,50 @@
     fim = g0[share:] + g1[:share]
     fwd_ref[0] = fre
     fwd_ref[1] = fim
+    if reduce_here:
+        row_gather.forward()
     kept = lax.broadcasted_iota(jnp.int32, (share, span), 1) < keep_ref[0]
     mre = jnp.where(kept, fre, 0.0).astype(jnp.bfloat16)
     mim = jnp.where(kept, fim, 0.0).astype(jnp.bfloat16)
     back = dot(rre, jnp.concatenate([mre, mim], 0), NT)
     back += dot(rim, jnp.concatenate([mim, -mre], 0), NT)
-    back_out[...] = back.astype(jnp.bfloat16).reshape(reps, tiles, ranks, 2 * share)
+    back = back.astype(jnp.bfloat16)
+    back_out[...] = back.reshape(reps, tiles, ranks, 2 * share)
 
     def back_copy(d):
         return tile_copy(back_out.at[:, lax.rem(t + d, tiles)], back_in.at[:, t], back_send, back_recv, d)
 
+    def red_copy(d):
+        return tile_copy(red_out.at[lax.rem(t + d, tiles)], red_in.at[t], red_send, red_recv, d)
+
+    def cor_copy(d):
+        return tile_copy(cor_all.at[t], cor_all.at[t], cor_send, cor_recv, d)
+
     each(1, tiles, lambda d: back_copy(d).start())
     back_in[:, t] = back_out[:, t]
+
+    if reduce_here:
+        row_gather.wait_recv()
+        both = dot(back, near_all[...].reshape(rows, 2 * reps * share), TN)
+        points = reps * share
+        part_re = both[:share, :points] + both[share:, points:]
+        part_im = both[share:, :points] - both[:share, points:]
+        part = jnp.concatenate([part_re, part_im], 0).astype(jnp.bfloat16)
+        red_out[...] = part.reshape(red_out.shape)
+        each(1, tiles, lambda d: red_copy(d).start())
+        red_in[t] = red_out[t]
+
+    sb_gather.forward()
+    each(1, tiles, lambda d: back_copy(d).wait_recv())
+    if reduce_here:
+        each(1, tiles, lambda d: red_copy(d).wait_recv())
+        total = red_in[0].astype(jnp.float32)
+        for j in range(1, tiles):
+            total += red_in[j].astype(jnp.float32)
+        cor_all[t] = (factor * total).astype(jnp.bfloat16)
+        each(1, tiles, lambda d: cor_copy(d).start())
+
     sb_gather.wait_recv()
-    each(1, tiles, lambda d: back_copy(d).wait_recv())
-
     arrived = back_in[...].reshape(rows, 2 * share)
     h0 = dot(arrived, sb_all[:, 0].reshape(rows, span), TN)
     h1 = dot(arrived, sb_all[:, 1].reshape(rows, span), TN)
@@ -164,37 +207,20 @@
     mar_ref[0] = are
     mar_ref[1] = aim
 
-    are = are.astype(jnp.bfloat16)
-    aim = aim.astype(jnp.bfloat16)
-    part_re = dot(are, foc_ref[0], NT) + dot(aim, foc_ref[1], NT)
-    part_im = dot(aim, foc_ref[0], NT) - dot(are, foc_ref[1], NT)
-    if reduce_here:
-        part = jnp.concatenate([part_re, part_im], 0).astype(jnp.bfloat16)
-        red_out[...] = part.reshape(red_out.shape)
-
-        def red_copy(d):
-            return tile_copy(red_out.at[lax.rem(t + d, tiles)], red_in.at[t], red_send, red_recv, d)
-
-        def cor_copy(d):
-            return tile_copy(cor_all.at[t], cor_all.at[t], cor_send, cor_recv, d)
-
-        each(1, tiles, lambda d: red_copy(d).start())
-        red_in[t] = red_out[t]
-        each(1, tiles, lambda d: red_copy(d).wait_recv())
-        total = red_in[0].astype(jnp.float32)
-        for j in range(1, tiles):
-            total += red_in[j].astype(jnp.float32)
-        cor_all[t] = (factor * total).astype(jnp.bfloat16)
-        each(1, tiles, lambda d: cor_copy(d).start())
+    if reduce_here:
+        each(1, count, lambda d: coef_copy(d).wait_send())
+        each(1, tiles, lambda d: near_copy(d).wait_send())
+        each(1, tiles, lambda d: red_copy(d).wait_send())
+        row_gather.wait_send()
         each(1, tiles, lambda d: cor_copy(d).wait_recv())
         cor_ref[...] = cor_all[...].astype(jnp.float32).reshape(cor_ref.shape)
-        each(1, tiles, lambda d: red_copy(d).wait_send())
         each(1, tiles, lambda d: cor_copy(d).wait_send())
     else:
-        cor_ref[0] = factor * part_re
-        cor_ref[1] = factor * part_im
-
-    each(1, count, lambda d: coef_copy(d).wait_send())
+        are = are.astype(jnp.bfloat16)
+        aim = aim.astype(jnp.bfloat16)
+        cor_ref[0] = factor * (dot(are, foc_ref[0], NT) + dot(aim, foc_ref[1], NT))
+        cor_ref[1] = factor * (dot(aim, foc_ref[0], NT) - dot(are, foc_ref[1], NT))
+        each(1, count, lambda d: coef_copy(d).wait_send())
     rb_gather.wait_send()
     sb_gather.wait_send()
     each(1, tiles, lambda d: back_copy(d).wait_send())
@@ -208,6 +234,7 @@
     factor = 1.0 / math.sqrt(SPAN * span * tiles)
     reduce_here = (2 * share) % (16 * tiles) == 0
     chunk = 2 * share // tiles if reduce_here else 16
+    near = (tiles, ranks, 2 * points) if reduce_here else (1, 16, 128)
     bf = jnp.bfloat16
     dma = pltpu.SemaphoreType.DMA
     smem = pl.BlockSpec(memory_space=pltpu.SMEM)
@@ -233,6 +260,10 @@
             pltpu.VMEM((tiles, chunk, points), bf),
             pltpu.VMEM((tiles, chunk, points), bf),
             pltpu.VMEM((tiles, chunk, points), bf),
+            pltpu.VMEM(near, bf),
+            pltpu.VMEM(near, bf),
+            pltpu.VMEM((reps,) + near, bf),
+            dma((tiles,)), dma((tiles,)), dma((reps,)), dma((reps,)),
             dma((tiles * reps,)), dma((tiles * reps,)),
             dma((reps,)), dma((reps,)), dma((reps,)), dma((reps,)),
             dma((tiles,)), dma((tiles,)), dma((tiles,)), dma((tiles,)), dma((tiles,)), dma((tiles,)),

time: 29.7 us -> 29.7 us (level)
  no operation moved by 1% of the time
where the time goes in v3:
time: 29.7 us; the launch traced here: 29.6 us
  Pallas kernels  25.1 us (85%)
  local copies, waits for them, and re-layouts  3.21 us (11%)
  between operations  1.3 us (4%)
    pallas_call x1, Pallas kernels, per_device(): pl.pallas_call(functools.partial(kernel, tiles, reps, reduce_here, factor...  25.1 us
    unnamed x7, local copies, waits for them, and re-layouts  3.21 us

profile of v3, /device:TPU:0, one launch (start us, length us, event | category | flops | bytes accessed | tf_op | source)
XLA Modules:
  0.0 29.6 jit_solution(11807855702237328111)
XLA Ops:
  1.3 25.1 %shard_map.76 = (f32[2,64,256]{2,1,0:T(8,128)}, f32[2,64,256]{2,1,0:T(8,128)}, f32[2,64,256]{2,1,0:T(8,128)}) custom-call(bf16[2,256,256]{2,1,0:T(8,128)(2,1)} %foc_ref.1, bf16[2,16,4,256]{3,2,1,0:T(4,128)(2,1)} %source_ref.1, bf16[2,16,4,256]{3,2,1,0:T(4,128)(2,1)} %receiver_ref.1, s32[4]{0:T(128)} %bitcast.1, s32[1]{0:T(128)S(6)} %copy.11.keep_ref), custom_call_target="tpu_custom_call" | custom-call | tf_op jit(solution)/shard_map/pallas_call | solution.py:242
  26.3 0.0 copy-start.1
  26.3 1.6 %copy.12 = f32[2,64,256]{2,1,0:T(8,128)} copy(f32[2,64,256]{2,1,0:T(8,128)} %get-tuple-element.6) | data formatting | bytes 262144
  28.0 0.0 copy-done.1
  28.0 0.0 copy-start
  28.0 0.7 %copy.13 = f32[2,64,256]{2,1,0:T(8,128)} copy(f32[2,64,256]{2,1,0:T(8,128)S(1)} %copy-done.1) | data formatting | bytes 262144
  28.6 0.3 copy-done
  28.9 0.7 %copy.14 = f32[2,64,256]{2,1,0:T(8,128)} copy(f32[2,64,256]{2,1,0:T(8,128)S(1)} %copy-done) | data formatting | bytes 262144
Async XLA Ops:
  26.3 1.6 %copy-start.1 = (f32[2,64,256]{2,1,0:T(8,128)S(1)}, f32[2,64,256]{2,1,0:T(8,128)}, u32[]{:S(2)}) copy-start(f32[2,64,256]{2,1,0:T(8,128)} %get-tuple-element.7) | copy-start | bytes 393220
  28.0 1.0 %copy-start = (f32[2,64,256]{2,1,0:T(8,128)S(1)}, f32[2,64,256]{2,1,0:T(8,128)}, u32[]{:S(2)}) copy-start(f32[2,64,256]{2,1,0:T(8,128)} %get-tuple-element.8) | copy-start | bytes 393220

commit v4 on v3

--- a/solution.py
+++ b/solution.py
@@ -29,9 +29,9 @@
         pl.loop(first, last)(body)
 
 
-def kernel(tiles, reps, reduce_here, factor, foc_ref, source_ref, receiver_ref, ranks_ref, keep_ref,
+def kernel(tiles, reps, reduce_here, factor, foc_hbm, source_hbm, receiver_hbm, ranks_ref, keep_ref,
            fwd_ref, mar_ref, cor_ref,
-           sb_ref, rb_ref, rb_all, sb_all, coef_out, coef_in, back_out, back_in, red_out, red_in, cor_all,
+           foc_ref, source_ref, receiver_ref, load_sem, sb_ref, rb_ref, rb_all, sb_all, coef_out, coef_in, back_out, back_in, red_out, red_in, cor_all,
            near_out, near_in, near_all,
            near_send, near_recv, row_send, row_recv,
            coef_send, coef_recv, rb_send, rb_recv, sb_send, sb_recv,
@@ -40,6 +40,8 @@
     r = lax.axis_index("rep")
     me = t * reps + r
     count = tiles * reps
+    loads = [pltpu.make_async_copy(src, dst, load_sem.at[i]) for i, (src, dst) in enumerate(
+        [(source_hbm, source_ref), (foc_hbm, foc_ref), (receiver_hbm, receiver_ref)])]
     ranks, span = sb_ref.shape[2], sb_ref.shape[3]
     share = foc_ref.shape[1] // reps
     rows = reps * tiles * ranks
@@ -48,6 +50,8 @@
         other = lax.rem(me + d, count)
         return other // reps, lax.rem(other, reps)
 
+    for c in loads:
+        c.start()
     barrier = pltpu.get_barrier_semaphore()
 
     def greet(d):
@@ -56,6 +60,8 @@
 
     each(1, count, greet)
 
+    for c in loads:
+        c.wait()
     bucket = (r * ranks + lax.broadcasted_iota(jnp.int32, (2, ranks, span), 1)) // BUCKET
     for a in range(tiles):
         wide = source_ref[:, :, a, :].astype(jnp.float32)
@@ -137,12 +143,12 @@
         near_out[...] = coef.astype(jnp.bfloat16).reshape(near_out.shape)
         each(1, tiles, lambda d: near_copy(d).start())
         near_in[t] = near_out[t]
-    sb_gather.start()
 
     rb_gather.forward()
     if reduce_here:
         each(1, tiles, lambda d: near_copy(d).wait_recv())
         row_gather.start()
+    sb_gather.start()
     rb_gather.wait_recv()
     each(1, count, lambda d: coef_copy(d).wait_recv())
 
@@ -153,8 +159,9 @@
     g1 = dot(arrived, rim, TN)
     fre = g0[:share] - g1[share:]
     fim = g0[share:] + g1[:share]
-    fwd_ref[0] = fre
-    fwd_ref[1] = fim
+    fwd_ref[0] = g0.reshape(2, share, span)
+    fwd_ref[1, 0] = -g1[share:]
+    fwd_ref[1, 1] = g1[:share]
     if reduce_here:
         row_gather.forward()
     kept = lax.broadcasted_iota(jnp.int32, (share, span), 1) < keep_ref[0]
@@ -188,24 +195,25 @@
         each(1, tiles, lambda d: red_copy(d).start())
         red_in[t] = red_out[t]
 
-    sb_gather.forward()
-    each(1, tiles, lambda d: back_copy(d).wait_recv())
     if reduce_here:
         each(1, tiles, lambda d: red_copy(d).wait_recv())
         total = red_in[0].astype(jnp.float32)
         for j in range(1, tiles):
             total += red_in[j].astype(jnp.float32)
-        cor_all[t] = (factor * total).astype(jnp.bfloat16)
+        cor_all[t] = total.astype(jnp.bfloat16)
         each(1, tiles, lambda d: cor_copy(d).start())
 
+    sb_gather.forward()
+    each(1, tiles, lambda d: back_copy(d).wait_recv())
     sb_gather.wait_recv()
     arrived = back_in[...].reshape(rows, 2 * share)
     h0 = dot(arrived, sb_all[:, 0].reshape(rows, span), TN)
     h1 = dot(arrived, sb_all[:, 1].reshape(rows, span), TN)
     are = h0[:share] + h1[share:]
     aim = h0[share:] - h1[:share]
-    mar_ref[0] = are
-    mar_ref[1] = aim
+    mar_ref[0] = h0.reshape(2, share, span)
+    mar_ref[1, 0] = h1[share:]
+    mar_ref[1, 1] = -h1[:share]
 
     if reduce_here:
         each(1, count, lambda d: coef_copy(d).wait_send())
@@ -213,13 +221,13 @@
         each(1, tiles, lambda d: red_copy(d).wait_send())
         row_gather.wait_send()
         each(1, tiles, lambda d: cor_copy(d).wait_recv())
-        cor_ref[...] = cor_all[...].astype(jnp.float32).reshape(cor_ref.shape)
+        cor_ref[...] = cor_all[...].reshape(cor_ref.shape)
         each(1, tiles, lambda d: cor_copy(d).wait_send())
     else:
         are = are.astype(jnp.bfloat16)
         aim = aim.astype(jnp.bfloat16)
-        cor_ref[0] = factor * (dot(are, foc_ref[0], NT) + dot(aim, foc_ref[1], NT))
-        cor_ref[1] = factor * (dot(aim, foc_ref[0], NT) - dot(are, foc_ref[1], NT))
+        cor_ref[0] = (dot(are, foc_ref[0], NT) + dot(aim, foc_ref[1], NT))
+        cor_ref[1] = (dot(aim, foc_ref[0], NT) - dot(are, foc_ref[1], NT))
         each(1, count, lambda d: coef_copy(d).wait_send())
     rb_gather.wait_send()
     sb_gather.wait_send()
@@ -237,18 +245,23 @@
     near = (tiles, ranks, 2 * points) if reduce_here else (1, 16, 128)
     bf = jnp.bfloat16
     dma = pltpu.SemaphoreType.DMA
+    anywhere = pl.BlockSpec(memory_space=pl.ANY)
     smem = pl.BlockSpec(memory_space=pltpu.SMEM)
     vmem = pl.BlockSpec(memory_space=pltpu.VMEM)
     fwd, mar, cor = pl.pallas_call(
         functools.partial(kernel, tiles, reps, reduce_here, factor),
         out_shape=(
-            jax.ShapeDtypeStruct((2, share, span), jnp.float32),
-            jax.ShapeDtypeStruct((2, share, span), jnp.float32),
-            jax.ShapeDtypeStruct((2, share, points), jnp.float32),
+            jax.ShapeDtypeStruct((2, 2, share, span), jnp.float32),
+            jax.ShapeDtypeStruct((2, 2, share, span), jnp.float32),
+            jax.ShapeDtypeStruct((2, share, points), bf if reduce_here else jnp.float32),
         ),
-        in_specs=[vmem, vmem, vmem, smem, smem],
+        in_specs=[anywhere, anywhere, anywhere, smem, smem],
         out_specs=(vmem, vmem, vmem),
         scratch_shapes=[
+            pltpu.VMEM(focusing.shape, bf),
+            pltpu.VMEM(source_basis.shape, bf),
+            pltpu.VMEM(receiver_basis.shape, bf),
+            dma((3,)),
             pltpu.VMEM((2, tiles, ranks, span), bf),
             pltpu.VMEM((2, tiles, ranks, span), bf),
             pltpu.VMEM((reps, 2, tiles, ranks, span), bf),
@@ -273,7 +286,7 @@
     )(focusing, source_basis, receiver_basis, tile_ranks.reshape(tiles), keep_counts)
     if not reduce_here:
         cor = lax.psum(cor, "tile")
-    return fwd, mar, cor
+    return fwd[0] + fwd[1], mar[0] + mar[1], factor * cor.astype(jnp.float32)
 
 
 def solution(mesh):

time: 29.7 us -> 28.9 us (0.973)
  local copies, waits for them, and re-layouts: 3.21 us -> 0.01 us
  other arithmetic: 0 us -> 2.52 us
    unnamed x7 -> x2, local copies, waits for them, and re-layouts: 3.21 us -> 0.01 us
    add x0 -> x1, other arithmetic: none -> 1.86 us  [per_device(): return (fwd[0] + fwd[1], mar[0] + mar[1], factor * cor.astype(jnp.float32))]
    mul x0 -> x1, other arithmetic: none -> 0.67 us  [per_device(): return (fwd[0] + fwd[1], mar[0] + mar[1], factor * cor.astype(jnp.float32))]
where the time goes in v4:
time: 28.9 us; the launch traced here: 28.8 us
  Pallas kernels  24.9 us (86%)
  other arithmetic  2.52 us (9%)
  between operations  1.29 us (4%)
    pallas_call x1, Pallas kernels, per_device(): pl.pallas_call(functools.partial(kernel, tiles, reps, reduce_here, factor...  24.9 us
    add x1, other arithmetic, per_device(): return (fwd[0] + fwd[1], mar[0] + mar[1], factor * cor.astype(jnp.float32))  1.86 us
    mul x1, other arithmetic, per_device(): return (fwd[0] + fwd[1], mar[0] + mar[1], factor * cor.astype(jnp.float32))  0.67 us

profile of v4, /device:TPU:0, one launch (start us, length us, event | category | flops | bytes accessed | tf_op | source)
XLA Modules:
  0.0 28.8 jit_solution(7906693946107016761)
XLA Ops:
  1.3 24.9 %shard_map.76 = (f32[2,2,64,256]{3,2,1,0:T(8,128)}, f32[2,2,64,256]{3,2,1,0:T(8,128)}, bf16[2,64,256]{2,1,0:T(8,128)(2,1)}) custom-call(bf16[2,256,256]{2,1,0:T(8,128)(2,1)} %foc_hbm.1, bf16[2,16,4,256]{3,2,1,0:T(4,128)(2,1)} %source_hbm.1, bf16[2,16,4,256]{3,2,1,0:T(4,128)(2,1)} %receiver_hbm.1, s32[4]{0:T(128)} %bitcast.5, s32[1]{0:T(128)S(6)} %copy.8.keep_ref), custom_call_target="tpu_custom_call" | custom-call | tf_op jit(solution)/shard_map/pallas_call | solution.py:251
  26.2 0.0 copy-start
  26.2 1.9 %add_bitcast_fusion = (f32[2,64,256]{2,1,0:T(8,128)}, f32[2,64,256]{2,1,0:T(8,128)}) fusion(f32[2,2,64,256]{3,2,1,0:T(8,128)} %get-tuple-element.7, f32[2,2,64,256]{3,2,1,0:T(8,128)} %get-tuple-element.6), kind=kLoop, calls=%fused_computation.1 | loop fusion | flops 65536 | bytes 786432 | tf_op jit(solution)/shard_map/add | solution.py:289
  28.1 0.0 copy-done
  28.1 0.7 %convert_multiply_fusion = f32[2,64,256]{2,1,0:T(8,128)} fusion(bf16[2,64,256]{2,1,0:T(8,128)(2,1)S(1)} %copy-done), kind=kLoop, calls=%fused_computation | loop fusion | flops 65536 | bytes 196608 | tf_op jit(solution)/shard_map/mul | solution.py:289
Async XLA Ops:
  26.2 1.9 %copy-start = (bf16[2,64,256]{2,1,0:T(8,128)(2,1)S(1)}, bf16[2,64,256]{2,1,0:T(8,128)(2,1)}, u32[]{:S(2)}) copy-start(bf16[2,64,256]{2,1,0:T(8,128)(2,1)} %get-tuple-element.8) | copy-start | bytes 196612
